TPU v7x, 32 devices: a whole 2x2x4 slice. The times are simulated.
32 devices in a mesh: brow: 8 (over z, core), bcol: 4 (over y, x).
Axes of the slice: x: 2, y: 2, z: 4, core: 2. Of those that a mesh axis runs over, the one named last changes fastest.
Arguments:
- right_side: float32 [16384, 64], P(('brow', 'bcol')), may hold values from -36 to 36
- tiles: bfloat16 [64, 1, 512, 512], P(('brow', 'bcol')), may hold values from -0.03125 to 0.03125
- row_blocks: int32 [64], P(('brow', 'bcol')), may hold values from 0 to 31, as said below
- col_blocks: int32 [64, 1], P(('brow', 'bcol')), may hold values from 0 to 31, as said below
Outputs:
- solution: float32 [16384, 64], P(('brow', 'bcol'))
- residual: float32 [16384, 64], P(('brow', 'bcol'))
Inputs may be any that keep to these rules, and one draw needn't show every extreme that they name: `row_blocks`: the 2 row blocks of one device lie in different groups, the group of block b being b % 4. `col_blocks`: the tile columns of the device at bcol index j are blocks c with c % 4 == j, different within one row slot.
All inputs are finite; a program needn't handle non-finite values.
Results may differ from a plain program's by a relative error of at most 0.0061.
Values may be sent and summed in bfloat16 or wider, within the bound.
A program may use at most 128 MiB of HBM per device.

v0:
```python
import jax
import jax.numpy as jnp
from jax import lax
from jax.sharding import PartitionSpec as P

ITERS = 3


highest = lax.Precision.HIGHEST


def solve_spd(matrix, rhs):
    factor = jnp.linalg.cholesky(matrix)
    return jax.scipy.linalg.cho_solve((factor, True), rhs)


def gram_of(left, right):
    return jnp.dot(left.T, right, precision=highest)


def right_mult(vectors, coeffs):
    return jnp.einsum("...k,kl->...l", vectors, coeffs, precision=highest)


def shards(right_side, tiles, row_blocks, col_blocks):
    groups = lax.axis_size("bcol")
    gblocks = lax.axis_size("brow")
    tile, width = right_side.shape
    slots, per_row = col_blocks.shape
    flat = tile * width
    slot_group = row_blocks % groups
    slot_place = row_blocks // groups
    col_place = col_blocks // groups
    group_ids = jnp.arange(groups, dtype=jnp.int32)
    block_ids = jnp.arange(gblocks, dtype=jnp.int32)
    matches = slot_group[:, None] == group_ids[None, :]
    wanted = jnp.sum(jnp.where(matches, slot_place[:, None], 0), axis=0)
    active = jnp.any(matches, axis=0).astype(jnp.int32)
    asked = lax.all_to_all(
        jnp.stack([wanted, active], axis=1), "bcol", split_axis=0, concat_axis=0, tiled=True
    )
    send_pick = ((asked[:, 0:1] == block_ids[None, :]) & (asked[:, 1:2] == 1)).astype(jnp.float32)
    slot_pick = matches.astype(jnp.float32)
    col_pick = (col_place.reshape(-1)[:, None] == block_ids[None, :]).astype(jnp.float32)
    own_index = lax.axis_index("brow")
    field = lax.all_gather(right_side[None], "brow", axis=0, tiled=True)

    def own(vectors):
        return lax.dynamic_index_in_dim(vectors, own_index, 0, keepdims=False)

    solution = jnp.zeros_like(field)
    residual = field
    direction = field
    rr_now = lax.psum(gram_of(own(residual), own(residual)), ("brow", "bcol"))
    for step in range(ITERS):
        stacked = direction.astype(jnp.bfloat16).reshape(gblocks, flat)
        outgoing = jnp.dot(
            send_pick.astype(jnp.bfloat16), stacked, preferred_element_type=jnp.float32
        ).astype(jnp.bfloat16)
        arrived = lax.all_to_all(outgoing, "bcol", split_axis=0, concat_axis=0, tiled=True)
        row_dir = jnp.dot(
            slot_pick.astype(jnp.bfloat16), arrived, preferred_element_type=jnp.float32
        )
        row_dir = row_dir.astype(jnp.bfloat16).reshape(slots, tile, width)
        col_dir = jnp.dot(
            col_pick.astype(jnp.bfloat16), stacked, preferred_element_type=jnp.float32
        )
        col_dir = col_dir.astype(jnp.bfloat16).reshape(slots, per_row, tile, width)
        turned = jnp.einsum("scab,sak->scbk", tiles, row_dir, preferred_element_type=jnp.float32)
        direct = jnp.einsum("scab,scbk->sak", tiles, col_dir, preferred_element_type=jnp.float32)
        local = jnp.dot(col_pick.T, turned.reshape(slots * per_row, flat), precision=highest)
        pushing = jnp.dot(slot_pick.T, direct.reshape(slots, flat), precision=highest)
        returned = lax.all_to_all(pushing, "bcol", split_axis=0, concat_axis=0, tiled=True)
        local = local + jnp.dot(send_pick.T, returned, precision=highest)
        summed = lax.psum(local.reshape(gblocks, tile, width), "brow")
        image = 3.0 * direction + summed
        curve = lax.psum(gram_of(own(direction), own(image)), ("brow", "bcol"))
        alpha = solve_spd(curve, rr_now)
        solution = solution + right_mult(direction, alpha)
        residual = residual - right_mult(image, alpha)
        if step + 1 < ITERS:
            fresh = lax.psum(gram_of(own(residual), own(residual)), ("brow", "bcol"))
            beta = solve_spd(rr_now, fresh)
            direction = residual + right_mult(direction, beta)
            rr_now = fresh
    return (own(solution), own(residual))


def solution(mesh):
    placed = (
        P(("brow", "bcol"), None),
        P(("brow", "bcol"), None, None, None),
        P(("brow", "bcol")),
        P(("brow", "bcol"), None),
    )
    return jax.shard_map(
        shards,
        mesh=mesh,
        in_specs=placed,
        out_specs=(P(("brow", "bcol"), None), P(("brow", "bcol"), None)),
        check_vma=False,
    )
```

profile of v0, /device:TPU:0, one launch (start us, length us, event | category | flops | bytes accessed | tf_op | source)
XLA Modules:
  0.0 629.2 jit_solution(16731248828745427380)
XLA Ops:
  9.4 5.2 all-to-all-start
  15.3 3.9 all-to-all-done
  19.4 15.1 %all-gather.3.cloned.1.call-done = f32[4096,64]{0,1:T(8,128)} async-done(((f32[512,64]{0,1:T(8,128)}), f32[4096,64]{0,1:T(8,128)}) %all-gather.3.cloned.1.call-update) | async-done | bytes 1048592 | tf_op jit(solution)/shard_map/all_gather | solution.py:46
  34.5 1.8 copy.235
  37.9 2.0 reshape.113
  43.1 3.6 all-to-all-start.1
  50.0 2.5 all-to-all-done.1
  52.5 4.1 all-to-all-start.2
  58.4 1.8 fusion.87
  60.2 3.8 all-to-all-done.2
  64.0 2.4 convolution_add_fusion.2
  66.4 2.2 reshape.119
  68.6 3.2 copy.173
  72.3 57.7 %all-reduce.5.cloned.1.call-done = f32[8,512,64]{1,2,0:T(8,128)} async-done(((f32[8,512,64]{1,2,0:T(8,128)}), f32[8,512,64]{1,2,0:T(8,128)}) %all-reduce.5.cloned.1.call-update) | async-done | bytes 1048592 | tf_op jit(solution)/shard_map/psum | solution.py:75
  131.8 40.2 %all-reduce = (f32[64,64]{0,1:T(8,128)S(1)}, f32[64,64]{0,1:T(8,128)S(1)}) all-reduce(f32[64,64]{0,1:T(8,128)S(1)} %fusion.29, f32[64,64]{0,1:T(8,128)S(1)} %fusion.31), channel_id=1, replica_groups=mesh['brow'=8,'bcol'=4] {'brow','bcol'}, use_global_device_ids=true, to_apply=%region_6.8 | all-reduce | flops 8192 | bytes 65536 | tf_op jit(solution)/shard_map/psum | solution.py:54
  172.2 5.8 cholesky.89
  179.3 4.9 custom-call.11
  187.4 40.0 %psum.66 = f32[64,64]{0,1:T(8,128)S(1)} all-reduce(f32[64,64]{0,1:T(8,128)S(1)} %fusion.41), channel_id=1, replica_groups=mesh['brow'=8,'bcol'=4] {'brow','bcol'}, use_global_device_ids=true, to_apply=%region_7.10 | all-reduce | flops 4096 | bytes 32768 | tf_op jit(solution)/shard_map/psum | solution.py:82
  227.4 5.8 cholesky.100
  234.6 4.9 custom-call.12
  240.0 3.1 fusion.102
  243.1 2.4 copy.185
  245.5 2.9 reshape.120
  248.3 2.0 convolution_convert_fusion.5
  250.4 2.0 fusion.1
  252.4 1.9 reduce.5
  255.3 4.6 all-to-all-start.3
  260.0 1.8 reshape.123
  261.8 2.1 convolution_bitcast_fusion.7
  264.0 2.0 copy.190
  265.9 2.0 reshape.124
  271.0 4.2 all-to-all-start.4
  282.2 1.8 fusion.86
  284.0 3.4 convolution_add_fusion.1
  287.3 3.4 reshape.125
  290.7 3.2 copy.192
  293.9 5.8 cholesky.122
  301.1 4.9 custom-call.14
  306.0 46.7 %all-reduce.7.cloned.1.call-done = f32[8,512,64]{1,2,0:T(8,128)} async-done(((f32[8,512,64]{1,2,0:T(8,128)}), f32[8,512,64]{1,2,0:T(8,128)}) %all-reduce.7.cloned.1.call-update) | async-done | bytes 1048592 | tf_op jit(solution)/shard_map/psum | solution.py:75
  355.4 39.6 %psum.68 = f32[64,64]{0,1:T(8,128)S(1)} all-reduce(f32[64,64]{0,1:T(8,128)S(1)} %fusion.38), channel_id=1, replica_groups=mesh['brow'=8,'bcol'=4] {'brow','bcol'}, use_global_device_ids=true, to_apply=%region_9.12 | all-reduce | flops 4096 | bytes 32768 | tf_op jit(solution)/shard_map/psum | solution.py:77
  395.2 5.8 cholesky.111
  402.3 4.9 custom-call.13
  408.4 2.7 convolution_subtract_fusion
  412.3 40.0 %psum.69 = f32[64,64]{1,0:T(8,128)S(1)} all-reduce(f32[64,64]{1,0:T(8,128)S(1)} %fusion.36), channel_id=1, replica_groups=mesh['brow'=8,'bcol'=4] {'brow','bcol'}, use_global_device_ids=true, to_apply=%region_10.13 | all-reduce | flops 4096 | bytes 32768 | tf_op jit(solution)/shard_map/psum | solution.py:82
  452.8 3.6 fusion.103
  456.4 2.4 copy.199
  458.8 2.9 reshape.126
  463.1 2.0 fusion.2
  465.1 1.9 reduce.6
  468.0 4.5 all-to-all-start.5
  473.4 2.1 convolution_bitcast_fusion.5
  475.5 1.9 copy.204
  477.4 2.0 reshape.130
  482.5 4.2 all-to-all-start.6
  495.8 3.3 convolution_add_fusion
  499.1 3.4 reshape.131
  502.5 3.2 copy.206
  505.7 2.0 convolution_bitcast_fusion.4
  507.8 2.1 fusion.104
  509.9 54.5 %all-reduce.9.cloned.1.call-done = f32[8,512,64]{1,2,0:T(8,128)} async-done(((f32[8,512,64]{1,2,0:T(8,128)}), f32[8,512,64]{1,2,0:T(8,128)}) %all-reduce.9.cloned.1.call-update) | async-done | bytes 1048592 | tf_op jit(solution)/shard_map/psum | solution.py:75
  566.2 39.4 %psum.71 = f32[64,64]{0,1:T(8,128)S(1)} all-reduce(f32[64,64]{0,1:T(8,128)S(1)} %fusion.33), channel_id=1, replica_groups=mesh['brow'=8,'bcol'=4] {'brow','bcol'}, use_global_device_ids=true, to_apply=%region_12.15 | all-reduce | flops 4096 | bytes 32768 | tf_op jit(solution)/shard_map/psum | solution.py:77
  605.7 5.8 cholesky.133
  612.9 4.9 custom-call.15
  620.5 1.8 fusion.27
  (137 shorter events, 62.1 us)
Async XLA Ops:
  7.2 39.7 %copy-start = (bf16[2,1,512,512]{3,2,1,0:T(8,128)(2,1)S(1)}, bf16[2,1,512,512]{3,2,1,0:T(8,128)(2,1)}, u32[]{:S(2)}) copy-start(bf16[2,1,512,512]{3,2,1,0:T(8,128)(2,1)} %param.8) | copy-start | bytes 3145732
  7.2 27.3 %all-gather.3.cloned.1.call-start = ((), (), s32[]{:S(2)}) async-start(), calls=%async_computation.10 | async-start | bytes 1179648 | tf_op jit(solution)/shard_map/all_gather | solution.py:46
  9.4 9.7 %all-to-all-start = ((s32[4,1,2]{2,1,0:T(1,128)}), s32[4,1,2]{2,1,0:T(1,128)S(1)}, u32[]{:S(2)}, u32[]{:S(2)}) async-start(s32[4,1,2]{2,1,0:T(1,128)} %copy.164), calls=%async_computation | async-start | bytes 4096 | tf_op jit(solution)/shard_map/all_to_all | solution.py:39
  43.1 9.4 %all-to-all-start.1 = ((bf16[4,2,16384]{2,1,0:T(2,128)(2,1)}), bf16[4,2,16384]{2,1,0:T(2,128)(2,1)S(1)}, u32[]{:S(2)}, u32[]{:S(2)}) async-start(bf16[4,2,16384]{2,1,0:T(2,128)(2,1)} %reshape.142), calls=%async_computation.1 | async-start | bytes 524288 | tf_op jit(solution)/shard_map/all_to_all | solution.py:60
  52.5 11.6 %all-to-all-start.2 = ((f32[4,1,32768]{2,1,0:T(1,128)}), f32[4,1,32768]{2,1,0:T(1,128)}, u32[]{:S(2)}, u32[]{:S(2)}) async-start(f32[4,1,32768]{2,1,0:T(1,128)} %copy.172), calls=%async_computation.2 | async-start | bytes 1048576 | tf_op jit(solution)/shard_map/all_to_all | solution.py:73
  56.6 73.4 %all-reduce.5.cloned.1.call-start = ((), (), s32[]{:S(2)}) async-start(), calls=%async_computation.7 | async-start | bytes 2097152 | tf_op jit(solution)/shard_map/psum | solution.py:75
  68.6 61.4 %copy-start.1 = (f32[4096,64]{0,1:T(8,128)S(1)}, f32[4096,64]{0,1:T(8,128)}, u32[]{:S(2)}) copy-start(f32[4096,64]{0,1:T(8,128)} %all-gather.3.cloned.1.call-done) | copy-start | bytes 3145732
  130.0 54.9 %copy-start.6 = (f32[8,512,64]{1,2,0:T(8,128)S(1)}, f32[8,512,64]{1,2,0:T(8,128)}, u32[]{:S(2)}) copy-start(f32[8,512,64]{1,2,0:T(8,128)} %all-reduce.5.cloned.1.call-done) | copy-start | bytes 3145732
  184.8 1.3 copy-start.7
  186.2 1.0 copy-start.2
  255.3 15.7 %all-to-all-start.3 = ((bf16[4,2,16384]{2,1,0:T(2,128)(2,1)}), bf16[4,2,16384]{2,1,0:T(2,128)(2,1)S(1)}, u32[]{:S(2)}, u32[]{:S(2)}) async-start(bf16[4,2,16384]{2,1,0:T(2,128)(2,1)} %reshape.144), calls=%async_computation.3 | async-start | bytes 524288 | tf_op jit(solution)/shard_map/all_to_all | solution.py:60
  271.0 13.0 %all-to-all-start.4 = ((f32[4,1,32768]{2,1,0:T(1,128)}), f32[4,1,32768]{2,1,0:T(1,128)}, u32[]{:S(2)}, u32[]{:S(2)}) async-start(f32[4,1,32768]{2,1,0:T(1,128)} %copy.191), calls=%async_computation.4 | async-start | bytes 1048576 | tf_op jit(solution)/shard_map/all_to_all | solution.py:73
  275.2 77.5 %all-reduce.7.cloned.1.call-start = ((), (), s32[]{:S(2)}) async-start(), calls=%async_computation.8 | async-start | bytes 2097152 | tf_op jit(solution)/shard_map/psum | solution.py:75
  354.2 1.0 copy-start.5
  407.7 0.6 copy-start.9
  411.1 1.0 copy-start.4
  452.3 6.4 %copy-start.11 = (f32[64,64]{1,0:T(8,128)}, f32[64,64]{1,0:T(8,128)S(1)}, u32[]{:S(2)}) copy-start(f32[64,64]{1,0:T(8,128)S(1)} %psum.69) | copy-start | bytes 49156
  468.0 14.5 %all-to-all-start.5 = ((bf16[4,2,16384]{2,1,0:T(2,128)(2,1)}), bf16[4,2,16384]{2,1,0:T(2,128)(2,1)S(1)}, u32[]{:S(2)}, u32[]{:S(2)}) async-start(bf16[4,2,16384]{2,1,0:T(2,128)(2,1)} %reshape.146), calls=%async_computation.5 | async-start | bytes 524288 | tf_op jit(solution)/shard_map/all_to_all | solution.py:60
  482.5 13.2 %all-to-all-start.6 = ((f32[4,1,32768]{2,1,0:T(1,128)}), f32[4,1,32768]{2,1,0:T(1,128)}, u32[]{:S(2)}, u32[]{:S(2)}) async-start(f32[4,1,32768]{2,1,0:T(1,128)} %copy.205), calls=%async_computation.6 | async-start | bytes 1048576 | tf_op jit(solution)/shard_map/all_to_all | solution.py:73
  486.7 77.7 %all-reduce.9.cloned.1.call-start = ((), (), s32[]{:S(2)}) async-start(), calls=%async_computation.9 | async-start | bytes 2097152 | tf_op jit(solution)/shard_map/psum | solution.py:75
  502.5 3.2 copy-start.8
  505.7 2.1 copy-start.10
  507.7 56.7 %copy-start.3 = (f32[8,512,64]{1,2,0:T(8,128)S(1)}, f32[8,512,64]{1,2,0:T(8,128)}, u32[]{:S(2)}) copy-start(f32[8,512,64]{1,2,0:T(8,128)} %get-tuple-element.11) | copy-start | bytes 3145732
  509.9 107.9 %copy-start.12 = (f32[64,64]{1,0:T(8,128)S(1)}, f32[64,64]{1,0:T(8,128)}, u32[]{:S(2)}) copy-start(f32[64,64]{1,0:T(8,128)} %copy-done.11) | copy-start | bytes 49156
Sparse Core Ops, SparseCore 0:
  9.6 24.7 all-gather.2
  72.0 57.9 all-reduce.4
  294.1 58.6 all-reduce.6
  505.8 58.5 all-reduce.8
where the time goes:
time: 639 us; the launch traced here: 629 us
  blocking collectives  199 us (31%)
  waiting for transfers between devices  185 us (29%)
  other arithmetic  73 us (11%)
  local copies, waits for them, and re-layouts  67.7 us (11%)
  matrix products  58.6 us (9%)
  starting transfers between devices  30.7 us (5%)
  between operations  14.9 us (2%)
    psum x3, waiting for transfers between devices, shards(): summed = lax.psum(local.reshape(gblocks, tile, width), 'brow')  159 us
    psum x2, blocking collectives, shards(): fresh = lax.psum(gram_of(own(residual), own(residual)), ('brow', 'bcol'))  80 us
    psum x2, blocking collectives, shards(): curve = lax.psum(gram_of(own(direction), own(image)), ('brow', 'bcol'))  79.1 us
    psum x1, blocking collectives, shards(): rr_now = lax.psum(gram_of(own(residual), own(residual)), ('brow', 'bcol'))  40.2 us
    another operation x15, other arithmetic, solve_spd(): factor = jnp.linalg.cholesky(matrix)  32.6 us
    another operation x10, other arithmetic, solve_spd(): return jax.scipy.linalg.cho_solve((factor, True), rhs)  27.7 us
    reshape x6, local copies, waits for them, and re-layouts, shards(): summed = lax.psum(local.reshape(gblocks, tile, width), 'brow')  18.6 us
    dot_general x8, matrix products, right_mult(): return jnp.einsum('...k,kl->...l', vectors, coeffs, precision=highest)  17 us
  transfers between devices with their start and end apart: 11, of which 7 were waited for; matrix products, arithmetic and copies ran while one was open for 10% of the time, Pallas kernels for 0%

commit v1 on v0

v1 whole, which is shorter than its diff:
```python
import functools

import jax
import jax.numpy as jnp
from jax import lax
from jax.experimental import pallas as pl
from jax.experimental.pallas import tpu as pltpu
from jax.sharding import PartitionSpec as P

ITERS = 3
CORES = 2
MESH = pl.DeviceIdType.MESH
highest = lax.Precision.HIGHEST


def dot32(left, right, dims):
    return lax.dot_general(
        left, right, (dims, ((), ())), precision=highest, preferred_element_type=jnp.float32
    )


def dot16(left, right, dims):
    return lax.dot_general(left, right, (dims, ((), ())), preferred_element_type=jnp.float32)


def kernel(
    chips, groups, slots, per_row,
    right_ref, tiles_ref, wants_ref, cols_ref, slot_ref,
    sol_ref, res_ref,
    dir_ref, image_ref, field, outgoing, arrived, pushing, returned, asked, direct, turned,
    core_out, core_in, z_own, z_out, z_in,
    gram, gram_in, part, part_in, total, left_sys, right_sys,
    z_sem, fwd_sem, ask_sem, out_sem, back_sem, core_sem, zs_sem, gr_sem, gx_sem, gg_sem,
):
    gblocks = chips * CORES
    width = right_ref.shape[0]
    brow = lax.axis_index("brow")
    bcol = lax.axis_index("bcol")
    z = brow // CORES
    core = lax.rem(brow, CORES)
    mate = 1 - core
    rows = 2 * width // gblocks

    def at_z(zz):
        return (zz * CORES + core, bcol)

    def at_row(row):
        return (row, bcol)

    def at_col(col):
        return (brow, col)

    barrier = pltpu.get_barrier_semaphore()
    for o in range(1, gblocks):
        pl.semaphore_signal(
            barrier, inc=1, device_id=at_row(lax.rem(brow + o, gblocks)), device_id_type=MESH
        )
    for o in range(1, groups):
        pl.semaphore_signal(
            barrier, inc=1, device_id=at_col(lax.rem(bcol + o, groups)), device_id_type=MESH
        )
    pl.semaphore_wait(barrier, gblocks + groups - 2)

    def send(src, dst, sems, slot, device):
        copy = pltpu.make_async_remote_copy(
            src_ref=src, dst_ref=dst, send_sem=sems.at[0, slot], recv_sem=sems.at[1, slot],
            device_id=device, device_id_type=MESH,
        )
        copy.start()
        return copy

    asks = []
    for o in range(1, groups):
        peer = lax.rem(bcol + o, groups)
        asks.append(send(wants_ref.at[peer], asked.at[bcol], ask_sem, o, at_col(peer)))
    asked[bcol] = wants_ref[bcol]

    res_ref[...] = right_ref[...]
    dir_ref[...] = right_ref[...]
    sol_ref[...] = jnp.zeros_like(sol_ref)

    def mixed(weights, count, value):
        acc = weights(0) * value(0).astype(jnp.float32)
        for k in range(1, count):
            acc = acc + weights(k) * value(k).astype(jnp.float32)
        return acc

    for step in range(ITERS):
        own = core * chips + z
        field[own] = dir_ref[...].astype(jnp.bfloat16)
        hops = []
        for o in range(1, chips):
            hops.append(
                send(field.at[own], field.at[own], z_sem, o, at_z(lax.rem(z + o, chips)))
            )
        forwards = [send(field.at[own], field.at[own], fwd_sem, 0, (z * CORES + mate, bcol))]
        for o in range(1, chips):
            hops[o - 1].wait_recv()
            src = core * chips + lax.rem(z - o + chips, chips)
            forwards.append(
                send(field.at[src], field.at[src], fwd_sem, o, (z * CORES + mate, bcol))
            )
        if step == 0:
            for copy in asks:
                copy.wait()
        for copy in hops:
            copy.wait_send()
        for copy in forwards:
            copy.wait()

        outs = []
        for o in range(1, groups + 1):
            peer = lax.rem(bcol + o, groups)
            picked = mixed(
                lambda k: asked[peer, pl.ds(k, 1), :], gblocks, lambda k: field[k]
            ).astype(jnp.bfloat16)
            if o < groups:
                outgoing[o] = picked
                outs.append(send(outgoing.at[o], arrived.at[bcol], out_sem, o, at_col(peer)))
            else:
                arrived[bcol] = picked

        def direct_of(s, carry):
            acc = jnp.zeros((width, tiles_ref.shape[2]), jnp.float32)
            for c in range(per_row):
                at = s * per_row + c
                picked = mixed(
                    lambda k: cols_ref[at, pl.ds(k, 1), :], gblocks, lambda k: field[k]
                ).astype(jnp.bfloat16)
                acc = acc + dot16(picked, tiles_ref[s, c], ((1,), (1,)))
            direct[s] = acc
            return carry

        lax.fori_loop(0, slots, direct_of, 0)
        backs = []
        for o in range(1, groups + 1):
            peer = lax.rem(bcol + o, groups)
            picked = mixed(
                lambda s: slot_ref[s, pl.ds(peer, 1), :], slots, lambda s: direct[s]
            ).astype(jnp.bfloat16)
            if o < groups:
                pushing[o] = picked
                backs.append(send(pushing.at[o], returned.at[bcol], back_sem, o, at_col(peer)))
            else:
                returned[bcol] = picked
        for copy in outs:
            copy.wait()

        def turned_of(s, carry):
            picked = mixed(
                lambda g: slot_ref[s, pl.ds(g, 1), :], groups, lambda g: arrived[g]
            ).astype(jnp.bfloat16)
            for c in range(per_row):
                turned[s * per_row + c] = dot16(picked, tiles_ref[s, c], ((1,), (0,)))
            return carry

        lax.fori_loop(0, slots, turned_of, 0)
        for copy in backs:
            copy.wait()

        def term(place):
            return mixed(
                lambda t: cols_ref[t, pl.ds(place, 1), :], slots * per_row, lambda t: turned[t]
            ) + mixed(lambda g: asked[g, pl.ds(place, 1), :], groups, lambda g: returned[g])

        crossing = []
        for k in range(chips):
            core_out[k] = term(mate * chips + k).astype(jnp.bfloat16)
            crossing.append(
                send(core_out.at[k], core_in.at[k], core_sem, k, (z * CORES + mate, bcol))
            )
        for o in range(1, chips + 1):
            zz = lax.rem(z + o, chips)
            z_own[o - 1] = term(core * chips + zz)
        for copy in crossing:
            copy.wait()
        backs = []
        for o in range(1, chips):
            zz = lax.rem(z + o, chips)
            z_out[o] = (z_own[o - 1] + core_in[zz].astype(jnp.float32)).astype(jnp.bfloat16)
            backs.append(send(z_out.at[o], z_in.at[o], zs_sem, o, at_z(zz)))
        image = 3.0 * dir_ref[...] + z_own[chips - 1] + core_in[z].astype(jnp.float32)
        for copy in backs:
            copy.wait()
        for o in range(1, chips):
            image = image + z_in[o].astype(jnp.float32)
        image_ref[...] = image

        direction = dir_ref[...]
        residual = res_ref[...]
        over = ((1,), (1,))
        curve = 0.5 * (dot32(direction, image, over) + dot32(image, direction, over))
        gram[0:width, :] = jnp.concatenate([curve, dot32(residual, residual, over)], axis=1)
        gram[width:, :] = jnp.concatenate(
            [dot32(residual, image, over), dot32(image, image, over)], axis=1
        )

        copies = []
        for o in range(1, gblocks):
            peer = lax.rem(brow + o, gblocks)
            copies.append(
                send(
                    gram.at[pl.ds(pl.multiple_of(peer * rows, rows), rows), :],
                    gram_in.at[o], gr_sem, o, at_row(peer),
                )
            )
        acc = gram[pl.ds(pl.multiple_of(brow * rows, rows), rows), :]
        for copy in copies:
            copy.wait()
        for o in range(1, gblocks):
            acc = acc + gram_in[o]
        part[...] = acc
        part_in[bcol] = acc
        copies = []
        for o in range(1, groups):
            copies.append(
                send(part, part_in.at[bcol], gx_sem, o, at_col(lax.rem(bcol + o, groups)))
            )
        for copy in copies:
            copy.wait()
        acc = part_in[0]
        for g in range(1, groups):
            acc = acc + part_in[g]
        mine = pl.ds(pl.multiple_of(brow * rows, rows), rows)
        total[mine, :] = acc
        copies = []
        for o in range(1, gblocks):
            copies.append(
                send(
                    total.at[mine, :], total.at[mine, :], gg_sem, o,
                    at_row(lax.rem(brow + o, gblocks)),
                )
            )
        for copy in copies:
            copy.wait()

        last = step + 1 == ITERS
        lanes = lax.broadcasted_iota(jnp.int32, (width, 2 * width), 1)
        subs = lax.broadcasted_iota(jnp.int32, (width, 2 * width), 0)
        top = total[0:width, :]
        left_sys[...] = top
        if not last:
            rr_now = top[:, width:]
            bottom = total[width:, :]
            eye = (lanes[:, :width] == subs[:, :width]).astype(jnp.float32)
            right_sys[...] = jnp.concatenate([rr_now, eye], axis=1)

        def eliminate(k, carry):
            for system in (left_sys,) if last else (left_sys, right_sys):
                whole = system[...]
                row = system[pl.ds(k, 1), :]
                pivot = jnp.sum(jnp.where(lanes[0:1, :] == k, row, 0.0), axis=1, keepdims=True)
                col = jnp.sum(jnp.where(lanes == k, whole, 0.0), axis=1, keepdims=True)
                scaled = row / pivot
                system[...] = jnp.where(subs == k, scaled, whole - col * scaled)
            return carry

        lax.fori_loop(0, width, eliminate, 0)
        alpha = left_sys[...][:, width:]
        flip = ((0,), (0,))
        sol_ref[...] = sol_ref[...] + dot32(alpha, direction, flip)
        residual = residual - dot32(alpha, image_ref[...], flip)
        res_ref[...] = residual
        if not last:
            cross = dot32(bottom[:, :width], alpha, ((1,), (0,)))
            square = dot32(alpha, dot32(bottom[:, width:], alpha, ((1,), (0,))), flip)
            fresh = rr_now - cross - cross.T + square
            beta = dot32(right_sys[...][:, width:], fresh, ((1,), (0,)))
            dir_ref[...] = residual + dot32(beta, direction, flip)


def shards(right_side, tiles, row_blocks, col_blocks):
    groups = lax.axis_size("bcol")
    gblocks = lax.axis_size("brow")
    chips = gblocks // CORES
    tile, width = right_side.shape
    slots, per_row = col_blocks.shape

    def place_of(blocks):
        place = blocks // groups
        return (place % CORES) * chips + place // CORES

    def wide(hot):
        return jnp.broadcast_to(hot.astype(jnp.float32)[..., None], hot.shape + (tile,))

    group_ids = jnp.arange(groups, dtype=jnp.int32)
    place_ids = jnp.arange(gblocks, dtype=jnp.int32)
    matches = (row_blocks % groups)[:, None] == group_ids[None, :]
    at_place = place_of(row_blocks)[:, None] == place_ids[None, :]
    wants = wide(jnp.any(matches[:, :, None] & at_place[:, None, :], axis=0))
    cols = wide(place_of(col_blocks.reshape(-1))[:, None] == place_ids[None, :])
    slot_hot = wide(matches)

    half = jnp.bfloat16
    full = jnp.float32
    rows = 2 * width // gblocks
    vec = (width, tile)
    dma = pltpu.SemaphoreType.DMA
    scratch = [
        pltpu.VMEM(vec, full), pltpu.VMEM(vec, full),
        pltpu.VMEM((gblocks,) + vec, half),
        pltpu.VMEM((groups,) + vec, half), pltpu.VMEM((groups,) + vec, half),
        pltpu.VMEM((groups,) + vec, half), pltpu.VMEM((groups,) + vec, half),
        pltpu.VMEM((groups, gblocks, tile), full),
        pltpu.VMEM((slots,) + vec, full), pltpu.VMEM((slots * per_row,) + vec, full),
        pltpu.VMEM((chips,) + vec, half), pltpu.VMEM((chips,) + vec, half),
        pltpu.VMEM((chips,) + vec, full),
        pltpu.VMEM((chips,) + vec, half), pltpu.VMEM((chips,) + vec, half),
        pltpu.VMEM((2 * width, 2 * width), full),
        pltpu.VMEM((gblocks, rows, 2 * width), full),
        pltpu.VMEM((rows, 2 * width), full),
        pltpu.VMEM((groups, rows, 2 * width), full),
        pltpu.VMEM((2 * width, 2 * width), full),
        pltpu.VMEM((width, 2 * width), full), pltpu.VMEM((width, 2 * width), full),
        dma((2, chips)), dma((2, chips)), dma((2, groups)), dma((2, groups)),
        dma((2, groups)), dma((2, chips)), dma((2, chips)),
        dma((2, gblocks)), dma((2, groups)), dma((2, gblocks)),
    ]
    whole = pl.BlockSpec(memory_space=pltpu.VMEM)
    solved, left = pl.pallas_call(
        functools.partial(kernel, chips, groups, slots, per_row),
        out_shape=(jax.ShapeDtypeStruct(vec, full), jax.ShapeDtypeStruct(vec, full)),
        in_specs=[whole] * 5,
        out_specs=(whole, whole),
        scratch_shapes=scratch,
        compiler_params=pltpu.CompilerParams(
            collective_id=0, has_side_effects=True, vmem_limit_bytes=48 * 1024 * 1024
        ),
    )(right_side.T, tiles, wants, cols, slot_hot)
    return (solved.T, left.T)


def solution(mesh):
    placed = (
        P(("brow", "bcol"), None),
        P(("brow", "bcol"), None, None, None),
        P(("brow", "bcol")),
        P(("brow", "bcol"), None),
    )
    return jax.shard_map(
        shards,
        mesh=mesh,
        in_specs=placed,
        out_specs=(P(("brow", "bcol"), None), P(("brow", "bcol"), None)),
        check_vma=False,
    )
```

time: 639 us -> 144 us (0.23); the launches traced: 629 us -> 144 us
  blocking collectives: 199 us -> 0 us
  waiting for transfers between devices: 185 us -> 0 us
  Pallas kernels: 0 us -> 139 us
  other arithmetic: 73 us -> 1.01 us
  local copies, waits for them, and re-layouts: 67.7 us -> 3.4 us
  matrix products: 58.6 us -> 0 us
  starting transfers between devices: 30.7 us -> 0 us
  between operations: 14.9 us -> 0.66 us
    psum x5 -> x0, blocking collectives: 199 us -> none  [the longest x2 80 us: shards(): fresh = lax.psum(gram_of(own(residual), own(residual)), ('brow', 'bcol'))]
    psum x3 -> x0, waiting for transfers between devices: 159 us -> none  [shards(): summed = lax.psum(local.reshape(gblocks, tile, width), 'brow')]
    pallas_call x0 -> x1, Pallas kernels: none -> 139 us  [shards(): pl.pallas_call(functools.partial(kernel, chips, groups, slots, per_row),...]
    another operation x25 -> x0, other arithmetic: 60.3 us -> none  [the longest x15 32.6 us: solve_spd(): factor = jnp.linalg.cholesky(matrix)]
    dot_general x38 -> x0, matrix products: 56.2 us -> none  [the longest x8 17 us: right_mult(): return jnp.einsum('...k,kl->...l', vectors, coeffs, precision=highest)]
    reshape x18 -> x0, local copies, waits for them, and re-layouts: 35.6 us -> none  [the longest x6 18.6 us: shards(): summed = lax.psum(local.reshape(gblocks, tile, width), 'brow')]
    all_to_all x7 -> x0, starting transfers between devices: 30.4 us -> none  [the longest x3 12.7 us: shards(): lax.all_to_all(outgoing, 'bcol', split_axis=0, concat_axis=0, tiled=True)]
    all_gather x1 -> x0, waiting for transfers between devices: 15.1 us -> none  [shards(): field = lax.all_gather(right_side[None], 'brow', axis=0, tiled=True)]
  transfers between devices with their start and end apart: 11 -> 0, of which waited for: 7 -> 0; matrix products, arithmetic and copies ran while one was open for 10% -> 0% of each run, Pallas kernels for 0% -> 0%
where the time goes in v1:
time: 144 us
  Pallas kernels  139 us (97%)
  local copies, waits for them, and re-layouts  3.4 us (2%)
    pallas_call x1, Pallas kernels, shards(): pl.pallas_call(functools.partial(kernel, chips, groups, slots, per_row),...  139 us
    unnamed x8, local copies, waits for them, and re-layouts  3.18 us

profile of v1, /device:TPU:0, one launch (start us, length us, event | category | flops | bytes accessed | tf_op | source)
XLA Modules:
  0.0 143.7 jit_solution(12895469554546757735)
XLA Ops:
  0.6 0.0 copy-start.2
  0.6 0.0 copy-start.1
  0.6 0.6 copy-done.2
  1.3 0.1 compare_convert_fusion
  1.4 0.7 and_select_fusion.6
  2.1 0.1 iota_compare_fusion
  2.1 0.1 fusion.5
  2.2 0.1 and_reduce_fusion
  2.3 0.1 broadcast_in_dim.8.slot_ref
  2.4 0.1 broadcast_in_dim.7.cols_ref
  2.4 0.1 broadcast_in_dim.6.wants_ref
  2.5 0.0 copy-done.1
  2.5 0.0 copy-start
  2.5 1.2 copy-done
  3.7 138.6 %shard_map.59 = (f32[64,512]{1,0:T(8,128)S(1)}, f32[64,512]{1,0:T(8,128)S(1)}) custom-call(f32[64,512]{1,0:T(8,128)S(1)} %bitcast.5, bf16[2,1,512,512]{3,2,1,0:T(8,128)(2,1)S(1)} %copy-done, f32[4,8,512]{2,1,0:T(8,128)S(1)} %broadcast_in_dim.6.wants_ref, f32[2,8,512]{2,1,0:T(8,128)S(1)} %broadcast_in_dim.7.cols_ref, f32[2,4,512]{2,1,0:T(4,128)S(1)} %broadcast_in_dim.8.slot_ref), custom_call_target="tpu_custom_call" | custom-call | tf_op jit(solution)/shard_map/pallas_call | solution.py:320
  142.4 0.7 copy.8
  143.0 0.7 copy.9
  (2 shorter events, 0.0 us)
Async XLA Ops:
  0.6 0.7 copy-start.2
  0.6 1.9 %copy-start.1 = (f32[512,64]{0,1:T(8,128)S(1)}, f32[512,64]{0,1:T(8,128)}, u32[]{:S(2)}) copy-start(f32[512,64]{0,1:T(8,128)} %param.4) | copy-start | bytes 393220
  2.5 1.2 copy-start

commit v2 on v1

--- a/solution.py
+++ b/solution.py
@@ -165,7 +165,7 @@
 
         crossing = []
         for k in range(chips):
-            core_out[k] = term(mate * chips + k).astype(jnp.bfloat16)
+            core_out[k] = term(mate * chips + k)
             crossing.append(
                 send(core_out.at[k], core_in.at[k], core_sem, k, (z * CORES + mate, bcol))
             )
@@ -177,9 +177,9 @@
         backs = []
         for o in range(1, chips):
             zz = lax.rem(z + o, chips)
-            z_out[o] = (z_own[o - 1] + core_in[zz].astype(jnp.float32)).astype(jnp.bfloat16)
+            z_out[o] = (z_own[o - 1] + core_in[zz]).astype(jnp.bfloat16)
             backs.append(send(z_out.at[o], z_in.at[o], zs_sem, o, at_z(zz)))
-        image = 3.0 * dir_ref[...] + z_own[chips - 1] + core_in[z].astype(jnp.float32)
+        image = 3.0 * dir_ref[...] + z_own[chips - 1] + core_in[z]
         for copy in backs:
             copy.wait()
         for o in range(1, chips):
@@ -245,17 +245,37 @@
             eye = (lanes[:, :width] == subs[:, :width]).astype(jnp.float32)
             right_sys[...] = jnp.concatenate([rr_now, eye], axis=1)
 
-        def eliminate(k, carry):
+        sub8 = subs[0:8, :]
+        lane8 = lanes[0:8, :]
+
+        def eliminate(band_index, carry):
+            base = pl.multiple_of(band_index * 8, 8)
             for system in (left_sys,) if last else (left_sys, right_sys):
                 whole = system[...]
-                row = system[pl.ds(k, 1), :]
-                pivot = jnp.sum(jnp.where(lanes[0:1, :] == k, row, 0.0), axis=1, keepdims=True)
-                col = jnp.sum(jnp.where(lanes == k, whole, 0.0), axis=1, keepdims=True)
-                scaled = row / pivot
-                system[...] = jnp.where(subs == k, scaled, whole - col * scaled)
+                band = system[pl.ds(base, 8), :]
+                cols, inner = [], []
+                for m in range(8):
+                    cols.append(
+                        jnp.sum(jnp.where(lanes == base + m, whole, 0.0), axis=1, keepdims=True)
+                    )
+                    col = jnp.sum(jnp.where(lane8 == base + m, band, 0.0), axis=1, keepdims=True)
+                    inner.append(jnp.broadcast_to(col, band.shape))
+                for m in range(8):
+                    inverse = 1.0 / inner[m][m : m + 1, :]
+                    for later in range(m + 1, 8):
+                        scaled = inner[later][m : m + 1, :] * inverse
+                        inner[later] = jnp.where(
+                            sub8 == m, scaled, inner[later] - inner[m] * scaled
+                        )
+                    scaled = band[m : m + 1, :] * inverse
+                    band = jnp.where(sub8 == m, scaled, band - inner[m] * scaled)
+                for m in range(8):
+                    whole = whole - cols[m] * band[m : m + 1, :]
+                system[...] = whole
+                system[pl.ds(base, 8), :] = band
             return carry
 
-        lax.fori_loop(0, width, eliminate, 0)
+        lax.fori_loop(0, width // 8, eliminate, 0)
         alpha = left_sys[...][:, width:]
         flip = ((0,), (0,))
         sol_ref[...] = sol_ref[...] + dot32(alpha, direction, flip)
@@ -303,7 +323,7 @@
         pltpu.VMEM((groups,) + vec, half), pltpu.VMEM((groups,) + vec, half),
         pltpu.VMEM((groups, gblocks, tile), full),
         pltpu.VMEM((slots,) + vec, full), pltpu.VMEM((slots * per_row,) + vec, full),
-        pltpu.VMEM((chips,) + vec, half), pltpu.VMEM((chips,) + vec, half),
+        pltpu.VMEM((chips,) + vec, full), pltpu.VMEM((chips,) + vec, full),
         pltpu.VMEM((chips,) + vec, full),
         pltpu.VMEM((chips,) + vec, half), pltpu.VMEM((chips,) + vec, half),
         pltpu.VMEM((2 * width, 2 * width), full),

time: 144 us -> 132 us (0.917)
  Pallas kernels: 139 us -> 126 us
    pallas_call x1, Pallas kernels: 139 us -> 126 us  [shards(): pl.pallas_call(functools.partial(kernel, chips, groups, slots, per_row),...]
where the time goes in v2:
time: 132 us; the launch traced here: 131 us
  Pallas kernels  126 us (95%)
  local copies, waits for them, and re-layouts  3.4 us (3%)
    pallas_call x1, Pallas kernels, shards(): pl.pallas_call(functools.partial(kernel, chips, groups, slots, per_row),...  126 us
    unnamed x8, local copies, waits for them, and re-layouts  3.18 us

profile of v2, /device:TPU:0, one launch (start us, length us, event | category | flops | bytes accessed | tf_op | source)
XLA Modules:
  0.0 131.4 jit_solution(15714421104524447407)
XLA Ops:
  0.6 0.0 copy-start.2
  0.6 0.0 copy-start.1
  0.6 0.6 copy-done.2
  1.3 0.1 compare_convert_fusion
  1.4 0.7 and_select_fusion.6
  2.1 0.1 iota_compare_fusion
  2.1 0.1 fusion.5
  2.2 0.1 and_reduce_fusion
  2.3 0.1 broadcast_in_dim.8.slot_ref
  2.4 0.1 broadcast_in_dim.7.cols_ref
  2.4 0.1 broadcast_in_dim.6.wants_ref
  2.5 0.0 copy-done.1
  2.5 0.0 copy-start
  2.5 1.2 copy-done
  3.7 126.3 %shard_map.59 = (f32[64,512]{1,0:T(8,128)S(1)}, f32[64,512]{1,0:T(8,128)S(1)}) custom-call(f32[64,512]{1,0:T(8,128)S(1)} %bitcast.5, bf16[2,1,512,512]{3,2,1,0:T(8,128)(2,1)S(1)} %copy-done, f32[4,8,512]{2,1,0:T(8,128)S(1)} %broadcast_in_dim.6.wants_ref, f32[2,8,512]{2,1,0:T(8,128)S(1)} %broadcast_in_dim.7.cols_ref, f32[2,4,512]{2,1,0:T(4,128)S(1)} %broadcast_in_dim.8.slot_ref), custom_call_target="tpu_custom_call" | custom-call | tf_op jit(solution)/shard_map/pallas_call | solution.py:340
  130.1 0.7 copy.8
  130.7 0.7 copy.9
  (2 shorter events, 0.0 us)
Async XLA Ops:
  0.6 0.7 copy-start.2
  0.6 1.9 %copy-start.1 = (f32[512,64]{0,1:T(8,128)S(1)}, f32[512,64]{0,1:T(8,128)}, u32[]{:S(2)}) copy-start(f32[512,64]{0,1:T(8,128)} %param.4) | copy-start | bytes 393220
  2.5 1.2 copy-start

commit v3 on v2

--- a/solution.py
+++ b/solution.py
@@ -28,7 +28,7 @@
     right_ref, tiles_ref, wants_ref, cols_ref, slot_ref,
     sol_ref, res_ref,
     dir_ref, image_ref, field, outgoing, arrived, pushing, returned, asked, direct, turned,
-    core_out, core_in, z_own, z_out, z_in,
+    core_out, core_in, z_out, z_in,
     gram, gram_in, part, part_in, total, left_sys, right_sys,
     z_sem, fwd_sem, ask_sem, out_sem, back_sem, core_sem, zs_sem, gr_sem, gx_sem, gg_sem,
 ):
@@ -103,6 +103,17 @@
         if step == 0:
             for copy in asks:
                 copy.wait()
+
+        def half_of(peer, side):
+            return mixed(
+                lambda k: asked[peer, pl.ds(side * chips + k, 1), :],
+                chips,
+                lambda k: field[side * chips + k],
+            )
+
+        for o in range(1, groups + 1):
+            peer = lax.rem(bcol + o, groups)
+            outgoing[o % groups] = half_of(peer, core).astype(jnp.bfloat16)
         for copy in hops:
             copy.wait_send()
         for copy in forwards:
@@ -111,9 +122,8 @@
         outs = []
         for o in range(1, groups + 1):
             peer = lax.rem(bcol + o, groups)
-            picked = mixed(
-                lambda k: asked[peer, pl.ds(k, 1), :], gblocks, lambda k: field[k]
-            ).astype(jnp.bfloat16)
+            picked = outgoing[o % groups].astype(jnp.float32) + half_of(peer, mate)
+            picked = picked.astype(jnp.bfloat16)
             if o < groups:
                 outgoing[o] = picked
                 outs.append(send(outgoing.at[o], arrived.at[bcol], out_sem, o, at_col(peer)))
@@ -164,22 +174,24 @@
             ) + mixed(lambda g: asked[g, pl.ds(place, 1), :], groups, lambda g: returned[g])
 
         crossing = []
-        for k in range(chips):
-            core_out[k] = term(mate * chips + k)
+        for o in range(1, chips + 1):
+            core_out[o - 1] = term(mate * chips + lax.rem(z + o, chips))
             crossing.append(
-                send(core_out.at[k], core_in.at[k], core_sem, k, (z * CORES + mate, bcol))
-            )
-        for o in range(1, chips + 1):
-            zz = lax.rem(z + o, chips)
-            z_own[o - 1] = term(core * chips + zz)
-        for copy in crossing:
-            copy.wait()
+                send(
+                    core_out.at[o - 1], core_in.at[o - 1], core_sem, o - 1,
+                    (z * CORES + mate, bcol),
+                )
+            )
         backs = []
         for o in range(1, chips):
             zz = lax.rem(z + o, chips)
-            z_out[o] = (z_own[o - 1] + core_in[zz]).astype(jnp.bfloat16)
+            mine = term(core * chips + zz)
+            crossing[o - 1].wait()
+            z_out[o] = (mine + core_in[o - 1]).astype(jnp.bfloat16)
             backs.append(send(z_out.at[o], z_in.at[o], zs_sem, o, at_z(zz)))
-        image = 3.0 * dir_ref[...] + z_own[chips - 1] + core_in[z]
+        mine = term(core * chips + z)
+        crossing[chips - 1].wait()
+        image = 3.0 * dir_ref[...] + mine + core_in[chips - 1]
         for copy in backs:
             copy.wait()
         for o in range(1, chips):
@@ -191,9 +203,10 @@
         over = ((1,), (1,))
         curve = 0.5 * (dot32(direction, image, over) + dot32(image, direction, over))
         gram[0:width, :] = jnp.concatenate([curve, dot32(residual, residual, over)], axis=1)
-        gram[width:, :] = jnp.concatenate(
-            [dot32(residual, image, over), dot32(image, image, over)], axis=1
-        )
+        if step + 1 < ITERS:
+            gram[width:, :] = jnp.concatenate(
+                [dot32(residual, image, over), dot32(image, image, over)], axis=1
+            )
 
         copies = []
         for o in range(1, gblocks):
@@ -324,7 +337,6 @@
         pltpu.VMEM((groups, gblocks, tile), full),
         pltpu.VMEM((slots,) + vec, full), pltpu.VMEM((slots * per_row,) + vec, full),
         pltpu.VMEM((chips,) + vec, full), pltpu.VMEM((chips,) + vec, full),
-        pltpu.VMEM((chips,) + vec, full),
         pltpu.VMEM((chips,) + vec, half), pltpu.VMEM((chips,) + vec, half),
         pltpu.VMEM((2 * width, 2 * width), full),
         pltpu.VMEM((gblocks, rows, 2 * width), full),

time: 132 us -> 129 us (0.977)
  Pallas kernels: 126 us -> 124 us
    pallas_call x1, Pallas kernels: 126 us -> 124 us  [shards(): pl.pallas_call(functools.partial(kernel, chips, groups, slots, per_row),...]
where the time goes in v3:
time: 129 us
  Pallas kernels  124 us (96%)
  local copies, waits for them, and re-layouts  3.4 us (3%)
    pallas_call x1, Pallas kernels, shards(): pl.pallas_call(functools.partial(kernel, chips, groups, slots, per_row),...  124 us
    unnamed x8, local copies, waits for them, and re-layouts  3.18 us

profile of v3, /device:TPU:0, one launch (start us, length us, event | category | flops | bytes accessed | tf_op | source)
XLA Modules:
  0.0 129.3 jit_solution(6699119385628369081)
XLA Ops:
  0.6 0.0 copy-start.2
  0.6 0.0 copy-start.1
  0.6 0.6 copy-done.2
  1.3 0.1 compare_convert_fusion
  1.4 0.7 and_select_fusion.6
  2.1 0.1 iota_compare_fusion
  2.1 0.1 fusion.5
  2.2 0.1 and_reduce_fusion
  2.3 0.1 broadcast_in_dim.8.slot_ref
  2.4 0.1 broadcast_in_dim.7.cols_ref
  2.4 0.1 broadcast_in_dim.6.wants_ref
  2.5 0.0 copy-done.1
  2.5 0.0 copy-start
  2.5 1.2 copy-done
  3.7 124.2 %shard_map.59 = (f32[64,512]{1,0:T(8,128)S(1)}, f32[64,512]{1,0:T(8,128)S(1)}) custom-call(f32[64,512]{1,0:T(8,128)S(1)} %bitcast.5, bf16[2,1,512,512]{3,2,1,0:T(8,128)(2,1)S(1)} %copy-done, f32[4,8,512]{2,1,0:T(8,128)S(1)} %broadcast_in_dim.6.wants_ref, f32[2,8,512]{2,1,0:T(8,128)S(1)} %broadcast_in_dim.7.cols_ref, f32[2,4,512]{2,1,0:T(4,128)S(1)} %broadcast_in_dim.8.slot_ref), custom_call_target="tpu_custom_call" | custom-call | tf_op jit(solution)/shard_map/pallas_call | solution.py:352
  128.0 0.7 copy.8
  128.6 0.7 copy.9
  (2 shorter events, 0.0 us)
Async XLA Ops:
  0.6 0.7 copy-start.2
  0.6 1.9 %copy-start.1 = (f32[512,64]{0,1:T(8,128)S(1)}, f32[512,64]{0,1:T(8,128)}, u32[]{:S(2)}) copy-start(f32[512,64]{0,1:T(8,128)} %param.4) | copy-start | bytes 393220
  2.5 1.2 copy-start
